TPU v7x, 256 devices: a whole 4x4x8 slice. The times are simulated.
256 devices in a mesh: row: 8 (over z), col: 16 (over x, y), vox: 2 (over core).
Axes of the slice: x: 4, y: 4, z: 8, core: 2. Of those that a mesh axis runs over, the one named last changes fastest.
Arguments:
- maps: bfloat16 [16384, 2048], P(('row', 'col'), 'vox'), may hold values from -21 to 21
- probes: bfloat16 [16384, 256], P(('row', 'col')), may hold values from -0.046875 to 0.046875
Outputs:
- gram: float32 [16384, 8, 16, 128], P('row', 'vox', 'col')
- basis: float32 [16384, 256], P(('row', 'col', 'vox'))
- factor: float32 [256, 256], replicated
All inputs are finite; a program needn't handle non-finite values.
Results may differ from a plain program's by a relative error of at most 0.004.
Values may be sent and summed in bfloat16 or wider, within the bound.
No kernel may reach another device: no remote copies, remote signals or barrier semaphores. Data moves between devices by JAX's collectives and lax.ppermute only.
A program may use at most 64 MiB of HBM per device.

v0:
```python
import jax
import jax.numpy as jnp
from jax import lax
from jax.sharding import PartitionSpec as P

VOX = 2048


def block_product(piece, partner):
    return (
        lax.dot_general(
            piece, partner, (((1,), (1,)), ((), ())), preferred_element_type=jnp.float32
        )
        / VOX
    )


def shards(maps, probes):
    sub_rows = maps.shape[0]
    row_count = lax.axis_size("row")
    col_count = lax.axis_size("col")
    vox_count = lax.axis_size("vox")
    subjects = sub_rows * row_count * col_count
    half_groups = row_count // vox_count
    vox_pos = lax.axis_index("vox")
    flat = maps.astype(jnp.float32)
    totals = lax.psum(jnp.sum(flat, axis=0), ("row", "col"))
    centered = (flat - totals[None, :] / subjects).astype(jnp.bfloat16)
    own_start = vox_pos * half_groups * sub_rows
    own_count = half_groups * sub_rows
    partial_sketch = None
    col_maps, col_probes = (
        lax.all_gather(centered, "row", axis=0, tiled=True),
        lax.all_gather(probes, "row", axis=0, tiled=True),
    )
    tile = block_product(lax.all_gather(centered, "col", axis=0, tiled=True), col_maps)
    block_rows = tile.shape[0]
    gram = lax.psum_scatter(
        tile.reshape(block_rows, row_count, 1, sub_rows), "vox", scatter_dimension=1, tiled=True
    )
    own_probes = lax.dynamic_slice_in_dim(col_probes, own_start, own_count, 0)
    partial_sketch = jnp.dot(
        gram.reshape(block_rows, own_count),
        own_probes.astype(jnp.float32),
        precision=lax.Precision.HIGHEST,
    )
    sketch = lax.psum_scatter(partial_sketch, ("col", "vox"), scatter_dimension=0, tiled=True)
    local_cross = lax.dot_general(
        sketch, sketch, (((0,), (0,)), ((), ())), precision=lax.Precision.HIGHEST
    )
    cross = lax.psum(local_cross, ("row", "col", "vox")) / subjects
    lower = jnp.linalg.cholesky(cross)
    basis = jax.scipy.linalg.solve_triangular(lower, sketch.T, lower=True).T
    return (gram, basis, lower.T)


def solution(mesh):
    placed = (P(("row", "col"), "vox"), P(("row", "col"), None))
    return jax.shard_map(
        shards,
        mesh=mesh,
        in_specs=placed,
        out_specs=(P("row", "vox", "col", None), P(("row", "col", "vox"), None), P()),
        check_vma=False,
    )
```

profile of v0, /device:TPU:2, one launch (start us, length us, event | category | flops | bytes accessed | tf_op | source)
XLA Modules:
  0.0 926.2 jit_solution(6317984655225748700)
XLA Ops:
  7.2 1.0 convert_reduce_fusion
  8.2 342.4 %psum.14 = f32[1024]{0:T(1024)S(1)} all-reduce(f32[1024]{0:T(1024)S(1)} %convert_reduce_fusion), channel_id=1, replica_groups=mesh['row'=8,'col'=16,'vox'=2] {'row','col'}, use_global_device_ids=true, to_apply=%region_1.0 | all-reduce | flops 1024 | bytes 8192 | tf_op jit(solution)/shard_map/psum | solution.py:27
  350.6 1.7 fusion
  353.1 42.8 %all-gather.5.cloned.1.call-done = bf16[1024,1024]{1,0:T(8,128)(2,1)} async-done(((bf16[128,1024]{1,0:T(8,128)(2,1)}), bf16[1024,1024]{1,0:T(8,128)(2,1)}) %all-gather.5.cloned.1.call-update) | async-done | bytes 2097168 | tf_op jit(solution)/shard_map/all_gather | solution.py:33
  396.0 58.1 %all-gather.3.cloned.1.call-done = bf16[2048,1024]{1,0:T(8,128)(2,1)} async-done(((bf16[128,1024]{1,0:T(8,128)(2,1)}), bf16[2048,1024]{1,0:T(8,128)(2,1)}) %all-gather.3.cloned.1.call-update) | async-done | bytes 4194320 | tf_op jit(solution)/shard_map/all_gather | solution.py:36
  454.1 10.6 %convolution_multiply_fusion = f32[2048,1024]{0,1:T(8,128)} fusion(bf16[2048,1024]{1,0:T(8,128)(2,1)} %all-gather.3.cloned.1.call-done, bf16[1024,1024]{1,0:T(8,128)(2,1)} %all-gather.5.cloned.1.call-done), kind=kOutput, calls=%fused_computation.2 | convolution fusion | flops 4297064448 | bytes 14680064 | tf_op jit(solution)/shard_map/dot_general | solution.py:11
  464.7 9.1 copy.14
  474.7 26.8 %all_gather.11 = bf16[1024,256]{1,0:T(8,128)(2,1)S(1)} all-gather(bf16[128,256]{1,0:T(8,128)(2,1)S(1)} %copy-done.1), channel_id=1, replica_groups=mesh['row'=8,'col'=16,'vox'=2] {'row'}, dimensions={0}, use_global_device_ids=true | all-gather | bytes 589824 | tf_op jit(solution)/shard_map/all_gather | solution.py:34
  501.4 5.3 copy.15
  506.8 7.0 fusion.2
  514.0 84.6 %reduce-scatter.5.cloned.1.call-done = f32[64,256]{1,0:T(8,128)} async-done(((f32[2048,256]{1,0:T(8,128)}), f32[64,256]{1,0:T(8,128)}) %reduce-scatter.5.cloned.1.call-update) | async-done | bytes 65552 | tf_op jit(solution)/shard_map/reduce_scatter | solution.py:47
  598.6 2.0 fusion.15
  600.6 8.4 copy.18
  609.1 246.4 %all-reduce.3.cloned.1.call-done = f32[256,256]{0,1:T(8,128)} async-done(((f32[256,256]{0,1:T(8,128)}), f32[256,256]{0,1:T(8,128)}) %all-reduce.3.cloned.1.call-update) | async-done | bytes 262160 | tf_op jit(solution)/shard_map/psum | solution.py:51
  855.5 1.0 broadcast_multiply_fusion
  856.6 1.0 fusion.1
  857.6 11.7 %cholesky.50 = f32[128,128]{1,0:T(8,128)S(1)} custom-call(f32[128,128]{1,0:T(8,128)S(1)} %cholesky.118), custom_call_target="Cholesky" | custom-call | tf_op jit(solution)/shard_map/jit(cholesky)/cholesky | solution.py:52
  869.3 9.8 %custom-call.15 = f32[1,128,128]{1,2,0:T(8,128)S(1)} custom-call(f32[1,128,128]{2,1,0:T(8,128)S(1)} %get-tuple-element.35), custom_call_target="InvertDiagBlocksLowerTriangular" | custom-call | tf_op jit(solution)/shard_map/jit(cholesky)/cholesky | solution.py:52
  879.6 11.7 %cholesky.105 = f32[128,128]{1,0:T(8,128)S(1)} custom-call(f32[128,128]{1,0:T(8,128)S(1)} %convolution_subtract_fusion), custom_call_target="Cholesky" | custom-call | tf_op jit(solution)/shard_map/jit(cholesky)/cholesky | solution.py:52
  893.6 4.1 while.1
  894.2 1.4 bitcast_dynamic-update-slice_fusion.2
  896.2 1.4 bitcast_dynamic-update-slice_fusion.2
  897.7 19.9 %custom-call.16 = f32[2,128,128]{1,2,0:T(8,128)S(1)} custom-call(f32[2,128,128]{2,1,0:T(8,128)S(1)} %get-tuple-element.10), custom_call_target="InvertDiagBlocksLowerTriangular" | custom-call | tf_op jit(solution)/shard_map/jit(_solve_triangular)/triangular_solve | solution.py:53
  918.8 0.8 copy.19
  (36 shorter events, 5.9 us)
Async XLA Ops:
  7.2 388.8 %all-gather.5.cloned.1.call-start = ((), (), s32[]{:S(2)}) async-start(), calls=%async_computation.3 | async-start | bytes 2359296 | tf_op jit(solution)/shard_map/all_gather | solution.py:33
  352.3 101.7 %all-gather.3.cloned.1.call-start = ((), (), s32[]{:S(2)}) async-start(), calls=%async_computation.2 | async-start | bytes 4456448 | tf_op jit(solution)/shard_map/all_gather | solution.py:36
  353.1 148.3 %reduce-scatter.3.cloned.1.call-start = ((), (), s32[]{:S(2)}) async-start(), calls=%async_computation.4 | async-start | bytes 12582912 | tf_op jit(solution)/shard_map/reduce_scatter | solution.py:38
  473.8 0.8 copy-start.1
  473.9 124.7 %reduce-scatter.5.cloned.1.call-start = ((), (), s32[]{:S(2)}) async-start(), calls=%async_computation.5 | async-start | bytes 2162688 | tf_op jit(solution)/shard_map/reduce_scatter | solution.py:47
  513.8 341.7 %all-reduce.3.cloned.1.call-start = ((), (), s32[]{:S(2)}) async-start(), calls=%async_computation.6 | async-start | bytes 524288 | tf_op jit(solution)/shard_map/psum | solution.py:51
  609.1 308.5 %copy-start = (f32[64,256]{1,0:T(8,128)S(1)}, f32[64,256]{1,0:T(8,128)}, u32[]{:S(2)}) copy-start(f32[64,256]{1,0:T(8,128)} %reduce-scatter.5.cloned.1.call-done) | copy-start | bytes 196612
Sparse Core Ops, SparseCore 0:
  352.5 43.4 all-gather.4
  399.0 55.0 all-gather.2
  474.0 21.9 reduce-scatter.2
  513.9 84.6 reduce-scatter.4
  605.3 250.0 all-reduce.2
where the time goes:
time: 927 us; the launch traced here: 926 us
  waiting for transfers between devices  433 us (47%)
  blocking collectives  369 us (40%)
  other arithmetic  59.3 us (6%)
  local copies, waits for them, and re-layouts  28.8 us (3%)
  matrix products  20.7 us (2%)
  between operations  15.2 us (2%)
    psum x1, blocking collectives, shards(): totals = lax.psum(jnp.sum(flat, axis=0), ('row', 'col'))  342 us
    psum x1, waiting for transfers between devices, shards(): cross = lax.psum(local_cross, ('row', 'col', 'vox')) / subjects  246 us
    reduce_scatter x1, waiting for transfers between devices, shards(): lax.psum_scatter(partial_sketch, ('col', 'vox'), scatter_dimension=0, til...  84.6 us
    all_gather x1, waiting for transfers between devices, shards(): lax.all_gather(centered, 'col', axis=0, tiled=True)  58.1 us
    all_gather x1, waiting for transfers between devices, shards(): lax.all_gather(centered, 'row', axis=0, tiled=True)  42.8 us
    another operation x6, other arithmetic, shards(): lower = jnp.linalg.cholesky(cross)  34 us
    all_gather x1, blocking collectives, shards(): lax.all_gather(probes, 'row', axis=0, tiled=True)  26.8 us
    another operation x2, other arithmetic, shards(): basis = jax.scipy.linalg.solve_triangular(lower, sketch.T, lower=True).T  19.9 us
  transfers between devices with their start and end apart: 5, of which 4 were waited for; matrix products, arithmetic and copies ran while one was open for 1% of the time, Pallas kernels for 0%

commit v1 on v0

--- a/solution.py
+++ b/solution.py
@@ -24,7 +24,7 @@
     half_groups = row_count // vox_count
     vox_pos = lax.axis_index("vox")
     flat = maps.astype(jnp.float32)
-    totals = lax.psum(jnp.sum(flat, axis=0), ("row", "col"))
+    totals = lax.psum(lax.psum(jnp.sum(flat, axis=0), "row"), "col")
     centered = (flat - totals[None, :] / subjects).astype(jnp.bfloat16)
     own_start = vox_pos * half_groups * sub_rows
     own_count = half_groups * sub_rows

time: 927 us -> 636 us (0.69)
  blocking collectives: 369 us -> 81.4 us
    psum x1 -> x2, blocking collectives: 342 us -> 54.6 us  [shards(): totals = lax.psum(lax.psum(jnp.sum(flat, axis=0), 'row'), 'col')]
where the time goes in v1:
time: 636 us; the launch traced here: 635 us
  waiting for transfers between devices  429 us (67%)
  blocking collectives  81.4 us (13%)
  other arithmetic  59.3 us (9%)
  local copies, waits for them, and re-layouts  28.8 us (5%)
  matrix products  20.7 us (3%)
  between operations  15.2 us (2%)
    psum x1, waiting for transfers between devices, shards(): cross = lax.psum(local_cross, ('row', 'col', 'vox')) / subjects  246 us
    reduce_scatter x1, waiting for transfers between devices, shards(): lax.psum_scatter(partial_sketch, ('col', 'vox'), scatter_dimension=0, til...  84.6 us
    all_gather x1, waiting for transfers between devices, shards(): lax.all_gather(centered, 'col', axis=0, tiled=True)  58.1 us
    psum x2, blocking collectives, shards(): totals = lax.psum(lax.psum(jnp.sum(flat, axis=0), 'row'), 'col')  54.6 us
    all_gather x1, waiting for transfers between devices, shards(): lax.all_gather(centered, 'row', axis=0, tiled=True)  39.6 us
    another operation x6, other arithmetic, shards(): lower = jnp.linalg.cholesky(cross)  34 us
    all_gather x1, blocking collectives, shards(): lax.all_gather(probes, 'row', axis=0, tiled=True)  26.8 us
    another operation x2, other arithmetic, shards(): basis = jax.scipy.linalg.solve_triangular(lower, sketch.T, lower=True).T  19.9 us
  transfers between devices with their start and end apart: 5, of which 4 were waited for; matrix products, arithmetic and copies ran while one was open for 1% of the time, Pallas kernels for 0%

profile of v1, /device:TPU:2, one launch (start us, length us, event | category | flops | bytes accessed | tf_op | source)
XLA Modules:
  0.0 635.2 jit_solution(14529822880203112052)
XLA Ops:
  7.2 1.0 convert_reduce_fusion
  8.2 20.0 %psum.21 = f32[1024]{0:T(1024)S(1)} all-reduce(f32[1024]{0:T(1024)S(1)} %convert_reduce_fusion), channel_id=1, replica_groups=mesh['row'=8,'col'=16,'vox'=2] {'row'}, use_global_device_ids=true, to_apply=%region_1.0 | all-reduce | flops 1024 | bytes 8192 | tf_op jit(solution)/shard_map/psum | solution.py:27
  28.2 34.6 %psum.22 = f32[1024]{0:T(1024)S(1)} all-reduce(f32[1024]{0:T(1024)S(1)} %psum.21), channel_id=1, replica_groups=mesh['row'=8,'col'=16,'vox'=2] {'col'}, use_global_device_ids=true, to_apply=%region_2.0 | all-reduce | flops 1024 | bytes 8192 | tf_op jit(solution)/shard_map/psum | solution.py:27
  62.8 1.7 fusion
  65.3 39.6 %all-gather.5.cloned.1.call-done = bf16[1024,1024]{1,0:T(8,128)(2,1)} async-done(((bf16[128,1024]{1,0:T(8,128)(2,1)}), bf16[1024,1024]{1,0:T(8,128)(2,1)}) %all-gather.5.cloned.1.call-update) | async-done | bytes 2097168 | tf_op jit(solution)/shard_map/all_gather | solution.py:33
  104.9 58.1 %all-gather.3.cloned.1.call-done = bf16[2048,1024]{1,0:T(8,128)(2,1)} async-done(((bf16[128,1024]{1,0:T(8,128)(2,1)}), bf16[2048,1024]{1,0:T(8,128)(2,1)}) %all-gather.3.cloned.1.call-update) | async-done | bytes 4194320 | tf_op jit(solution)/shard_map/all_gather | solution.py:36
  163.0 10.6 %convolution_multiply_fusion = f32[2048,1024]{0,1:T(8,128)} fusion(bf16[2048,1024]{1,0:T(8,128)(2,1)} %all-gather.3.cloned.1.call-done, bf16[1024,1024]{1,0:T(8,128)(2,1)} %all-gather.5.cloned.1.call-done), kind=kOutput, calls=%fused_computation.2 | convolution fusion | flops 4297064448 | bytes 14680064 | tf_op jit(solution)/shard_map/dot_general | solution.py:11
  173.7 9.1 %copy.14 = f32[2048,8,1,128]{3,0,2,1:T(8,128)} copy(f32[2048,8,1,128]{0,3,1,2:T(8,128)} %bitcast.44) | data formatting | bytes 16777216 | tf_op jit(solution)/shard_map/reshape | solution.py:39
  183.6 26.8 %all_gather.11 = bf16[1024,256]{1,0:T(8,128)(2,1)S(1)} all-gather(bf16[128,256]{1,0:T(8,128)(2,1)S(1)} %copy-done.1), channel_id=1, replica_groups=mesh['row'=8,'col'=16,'vox'=2] {'row'}, dimensions={0}, use_global_device_ids=true | all-gather | bytes 589824 | tf_op jit(solution)/shard_map/all_gather | solution.py:34
  210.4 5.3 copy.15
  215.7 7.0 %fusion.2 = f32[2048,256]{1,0:T(8,128)} fusion(f32[2048,512]{0,1:T(8,128)} %bitcast.43, bf16[1024,256]{1,0:T(8,128)(2,1)S(1)} %all_gather.11, s32[]{:T(128)S(6)} %select_n.7), kind=kOutput, calls=%fused_computation.11 | convolution fusion | flops 3221225472 | bytes 6553604 | tf_op jit(solution)/shard_map/dot_general | solution.py:42
  222.9 84.6 %reduce-scatter.5.cloned.1.call-done = f32[64,256]{1,0:T(8,128)} async-done(((f32[2048,256]{1,0:T(8,128)}), f32[64,256]{1,0:T(8,128)}) %reduce-scatter.5.cloned.1.call-update) | async-done | bytes 65552 | tf_op jit(solution)/shard_map/reduce_scatter | solution.py:47
  307.6 2.0 fusion.15
  309.6 8.4 %copy.18 = f32[2048,4,1,128]{3,2,1,0:T(1,128)} copy(f32[2048,4,1,128]{3,0,2,1:T(8,128)} %reduce-scatter.3.cloned.1.call-done) | data formatting | bytes 8388608
  318.1 246.3 %all-reduce.3.cloned.1.call-done = f32[256,256]{0,1:T(8,128)} async-done(((f32[256,256]{0,1:T(8,128)}), f32[256,256]{0,1:T(8,128)}) %all-reduce.3.cloned.1.call-update) | async-done | bytes 262160 | tf_op jit(solution)/shard_map/psum | solution.py:51
  564.4 1.0 broadcast_multiply_fusion
  565.5 1.0 fusion.1
  566.5 11.7 %cholesky.50 = f32[128,128]{1,0:T(8,128)S(1)} custom-call(f32[128,128]{1,0:T(8,128)S(1)} %cholesky.118), custom_call_target="Cholesky" | custom-call | tf_op jit(solution)/shard_map/jit(cholesky)/cholesky | solution.py:52
  578.3 9.8 %custom-call.15 = f32[1,128,128]{1,2,0:T(8,128)S(1)} custom-call(f32[1,128,128]{2,1,0:T(8,128)S(1)} %get-tuple-element.35), custom_call_target="InvertDiagBlocksLowerTriangular" | custom-call | tf_op jit(solution)/shard_map/jit(cholesky)/cholesky | solution.py:52
  588.6 11.7 %cholesky.105 = f32[128,128]{1,0:T(8,128)S(1)} custom-call(f32[128,128]{1,0:T(8,128)S(1)} %convolution_subtract_fusion), custom_call_target="Cholesky" | custom-call | tf_op jit(solution)/shard_map/jit(cholesky)/cholesky | solution.py:52
  602.5 4.1 while.1
  603.1 1.4 bitcast_dynamic-update-slice_fusion.2
  605.2 1.4 bitcast_dynamic-update-slice_fusion.2
  606.6 19.9 %custom-call.16 = f32[2,128,128]{1,2,0:T(8,128)S(1)} custom-call(f32[2,128,128]{2,1,0:T(8,128)S(1)} %get-tuple-element.10), custom_call_target="InvertDiagBlocksLowerTriangular" | custom-call | tf_op jit(solution)/shard_map/jit(_solve_triangular)/triangular_solve | solution.py:53
  (37 shorter events, 6.7 us)
Async XLA Ops:
  7.2 97.7 %all-gather.5.cloned.1.call-start = ((), (), s32[]{:S(2)}) async-start(), calls=%async_computation.3 | async-start | bytes 2359296 | tf_op jit(solution)/shard_map/all_gather | solution.py:33
  64.5 98.5 %all-gather.3.cloned.1.call-start = ((), (), s32[]{:S(2)}) async-start(), calls=%async_computation.2 | async-start | bytes 4456448 | tf_op jit(solution)/shard_map/all_gather | solution.py:36
  65.3 145.1 %reduce-scatter.3.cloned.1.call-start = ((), (), s32[]{:S(2)}) async-start(), calls=%async_computation.4 | async-start | bytes 12582912 | tf_op jit(solution)/shard_map/reduce_scatter | solution.py:38
  182.8 0.8 copy-start.1
  182.8 124.8 %reduce-scatter.5.cloned.1.call-start = ((), (), s32[]{:S(2)}) async-start(), calls=%async_computation.5 | async-start | bytes 2162688 | tf_op jit(solution)/shard_map/reduce_scatter | solution.py:47
  222.7 341.7 %all-reduce.3.cloned.1.call-start = ((), (), s32[]{:S(2)}) async-start(), calls=%async_computation.6 | async-start | bytes 524288 | tf_op jit(solution)/shard_map/psum | solution.py:51
  318.1 308.5 %copy-start = (f32[64,256]{1,0:T(8,128)S(1)}, f32[64,256]{1,0:T(8,128)}, u32[]{:S(2)}) copy-start(f32[64,256]{1,0:T(8,128)} %reduce-scatter.5.cloned.1.call-done) | copy-start | bytes 196612
Sparse Core Ops, SparseCore 0:
  64.7 40.1 all-gather.4
  107.9 55.0 all-gather.2
  182.9 21.9 reduce-scatter.2
  222.8 84.6 reduce-scatter.4
  314.3 250.0 all-reduce.2
